TPU v7x, 768 devices: a whole 4x8x12 slice. The times are simulated.
768 devices in a mesh: section: 32 (over y_hi, x, core), peer: 24 (over z, y_lo).
Axes of the slice: x: 4, y: 8 (y_hi: 4, y_lo: 2; y = y_hi * 2 + y_lo), z: 12, core: 2. Of those that a mesh axis runs over, the one named last changes fastest.
Arguments:
- stash: bfloat16 [32, 24, 18, 8, 5120], P('section', 'peer'), may hold values from -134 to 134
- back_in: bfloat16 [32, 24, 18, 8, 5120], P('section', 'peer'), may hold values from -6 to 6
- down_proj: bfloat16 [32, 144, 5120], P('section'), may hold values from -0.078125 to 0.078125
- up_proj: bfloat16 [32, 144, 5120], P('section'), may hold values from -0.5 to 0.5
- gain: float32 [32, 5120], P('section'), may hold values from 0.5 to 1.5
- sent_to: int32 [32, 24, 18], P('section', 'peer'), may hold values from 0 to 23, as said below
- sent_count: int32 [32, 24], P('section', 'peer'), may hold values from 14 to 18, as said below
- recv_from: int32 [32, 24, 18], P('section', 'peer'), may hold values from 0 to 23, as said below
- back_live: int32 [32, 24, 18], P('section', 'peer'), may hold values from 0 to 1, as said below
Outputs:
- returned: bfloat16 [32, 24, 18, 8, 5120], P('section', 'peer')
- grad_down: bfloat16 [32, 144, 5120], P('section')
- grad_up: bfloat16 [32, 144, 5120], P('section')
Inputs may be any that keep to these rules, and one draw needn't show every extreme that they name: `sent_to`: the 18 slots of one device name distinct peers. `sent_count`: uneven over peers; on every section some peer has 18. `recv_from`: the 18 slots of one device name distinct peers. Peer c of section s - 1 (the last section before section 0) names peer a of section s in one of its first sent_count slots exactly when some slot of recv_from at (s, a) names c with back_live 1. `back_live`: on every section some device has all 18 slots live.
All inputs are finite; a program needn't handle non-finite values.
Results may differ from a plain program's by a relative error of at most 0.028.
Values may be sent and summed in bfloat16 or wider, within the bound.
No kernel may reach another device: no remote copies, remote signals or barrier semaphores. Data moves between devices by JAX's collectives and lax.ppermute only.
A program may use at most 64 MiB of HBM per device.

v0:
```python
import jax
import jax.numpy as jnp
from jax import lax
from jax.sharding import PartitionSpec as P

epsilon = 1e-05


def passed_along(block, axis, distance):
    devices = range(lax.axis_size(axis))
    route = [((i - distance) % len(devices), i) for i in devices]
    return lax.ppermute(block, axis, route)


def compact(blocks, targets, live_count):
    peer_count = blocks.shape[0]
    send_slots = targets.shape[0]
    peer_index = jnp.arange(peer_count, dtype=jnp.int32)
    slot_index = jnp.arange(send_slots, dtype=jnp.int32)
    selector = (
        (targets[:, None] == peer_index[None, :]) & (slot_index[:, None] < live_count)
    ).astype(jnp.bfloat16)
    flat = blocks.reshape(peer_count, -1)
    packed = jnp.dot(selector, flat, preferred_element_type=jnp.float32).astype(jnp.bfloat16)
    return packed.reshape((send_slots,) + blocks.shape[1:])


def on_device(stash, back_in, down_proj, up_proj, gain, sent_to, sent_count, recv_from, back_live):
    peer_count = lax.axis_size("peer")
    live_slots = back_live[0, 0]
    slot_mask = live_slots.astype(jnp.bfloat16)[:, None, None]
    slot_count = stash.shape[2]
    micro_rows = stash.shape[3]
    model_width = stash.shape[4]
    stored = (stash[0, 0] * slot_mask).reshape(slot_count * micro_rows, model_width)
    incoming = (back_in[0, 0] * slot_mask).reshape(slot_count * micro_rows, model_width)
    section_gain = gain[0]
    down_local = down_proj[0]
    up_local = up_proj[0]
    stored_f = stored.astype(jnp.float32)
    inverse = lax.rsqrt(jnp.mean(stored_f * stored_f, axis=-1, keepdims=True) + epsilon)
    unit_rows = stored_f * inverse
    normed = (unit_rows * section_gain).astype(jnp.bfloat16)
    contract_last = (((1,), (1,)), ((), ()))
    contract_rows = (((0,), (0,)), ((), ()))
    preact = lax.dot_general(normed, down_local, contract_last, preferred_element_type=jnp.float32)
    sigmoid_pre = jax.nn.sigmoid(preact)
    activation = (preact * sigmoid_pre).astype(jnp.bfloat16)
    back_act = lax.dot_general(
        incoming, up_local, contract_last, preferred_element_type=jnp.float32
    )
    back_pre = (back_act * (sigmoid_pre * (1.0 + preact * (1.0 - sigmoid_pre)))).astype(
        jnp.bfloat16
    )
    back_norm = jnp.dot(back_pre, down_local, preferred_element_type=jnp.float32) * section_gain
    input_grad = incoming.astype(jnp.float32) + inverse * (
        back_norm - unit_rows * jnp.mean(back_norm * unit_rows, axis=-1, keepdims=True)
    )
    input_grad = input_grad.astype(jnp.bfloat16)
    peer_index = jnp.arange(peer_count, dtype=jnp.int32)
    spreader = (
        (recv_from[0, 0][None, :] == peer_index[:, None]) & (live_slots[None, :] == 1)
    ).astype(jnp.bfloat16)
    by_sender = jnp.dot(
        spreader, input_grad.reshape(slot_count, -1), preferred_element_type=jnp.float32
    ).astype(jnp.bfloat16)
    by_sender = by_sender.reshape(peer_count, micro_rows, model_width)
    exchanged = lax.all_to_all(by_sender, "peer", split_axis=0, concat_axis=0, tiled=True)
    arrived = passed_along(exchanged, "section", -1)
    returned = compact(arrived, sent_to[0, 0], sent_count[0, 0])
    part_down = (
        lax.dot_general(back_pre, normed, contract_rows, preferred_element_type=jnp.float32)
        .astype(jnp.bfloat16)
        .astype(jnp.float32)
    )
    part_up = (
        lax.dot_general(activation, incoming, contract_rows, preferred_element_type=jnp.float32)
        .astype(jnp.bfloat16)
        .astype(jnp.float32)
    )
    summed_down, summed_up = (
        lax.psum(part_down.astype(jnp.bfloat16), "peer").astype(jnp.float32),
        lax.psum(part_up.astype(jnp.bfloat16), "peer").astype(jnp.float32),
    )
    grad_down = (summed_down / peer_count).astype(jnp.bfloat16)
    grad_up = (summed_up / peer_count).astype(jnp.bfloat16)
    return (returned[None, None], grad_down[None], grad_up[None])


def solution(mesh):
    placed = (
        P("section", "peer", None, None, None),
        P("section", "peer", None, None, None),
        P("section", None, None),
        P("section", None, None),
        P("section", None),
        P("section", "peer", None),
        P("section", "peer"),
        P("section", "peer", None),
        P("section", "peer", None),
    )
    return jax.shard_map(
        on_device,
        mesh=mesh,
        in_specs=placed,
        out_specs=(
            P("section", "peer", None, None, None),
            P("section", None, None),
            P("section", None, None),
        ),
        check_vma=False,
    )
```

profile of v0, /device:TPU:16, one launch (start us, length us, event | category | flops | bytes accessed | tf_op | source)
XLA Modules:
  0.0 322.3 jit_solution(3411286279478968722)
XLA Ops:
  7.2 0.8 convert_bitcast_fusion
  8.0 0.7 compare_bitcast_fusion
  8.7 1.9 fusion
  10.8 0.1 mul.99
  11.0 0.7 fusion.6
  11.7 0.7 copy-done.2
  12.3 0.4 copy-done.7
  12.8 0.6 fusion.24
  13.4 1.0 multiply_reduce_fusion
  14.4 2.3 add_convert_fusion
  16.7 3.7 %reshape.93 = bf16[18,40960]{1,0:T(8,128)(2,1)} reshape(bf16[144,5120]{1,0:T(8,128)(2,1)} %add_convert_fusion) | data formatting | bytes 2949120 | tf_op jit(solution)/shard_map/reshape | solution.py:65
  20.4 2.2 convolution_convert_fusion.1
  22.6 2.3 copy.12
  24.9 16.5 %all-to-all-start = ((bf16[24,8,5120]{2,1,0:T(8,128)(2,1)}), bf16[24,8,5120]{2,1,0:T(8,128)(2,1)}, u32[]{:S(2)}, u32[]{:S(2)}) async-start(bf16[24,8,5120]{2,1,0:T(8,128)(2,1)} %bitcast.64), calls=%async_computation | async-start | bytes 3932160 | tf_op jit(solution)/shard_map/all_to_all | solution.py:68
  41.5 1.9 convolution_convert_fusion.3
  43.3 1.7 convolution_convert_fusion.2
  45.1 75.3 %all-to-all-done = bf16[24,8,5120]{2,1,0:T(8,128)(2,1)} async-done(((bf16[24,8,5120]{2,1,0:T(8,128)(2,1)}), bf16[24,8,5120]{2,1,0:T(8,128)(2,1)}, u32[]{:S(2)}, u32[]{:S(2)}) %all-to-all-start) | async-done | bytes 1966112 | tf_op jit(solution)/shard_map/all_to_all | solution.py:68
  120.3 1.9 collective-permute-start
  122.9 184.4 %all-reduce.3.cloned.1.call-done = (bf16[144,5120]{1,0:T(8,128)(2,1)}, bf16[144,5120]{1,0:T(8,128)(2,1)}) async-done(((bf16[144,5120]{1,0:T(8,128)(2,1)}, bf16[144,5120]{1,0:T(8,128)(2,1)}), (bf16[144,5120]{1,0:T(8,128)(2,1)}, bf16[144,5120]{1,0:T(8,128)(2,1)})) %all-reduce.3.cloned.1.call-update) | async-done | bytes 2949136 | tf_op jit(solution)/shard_map/psum | solution.py:82
  307.3 4.0 %fusion.3 = (bf16[1,144,5120]{2,1,0:T(8,128)(2,1)}, bf16[1,144,5120]{2,1,0:T(8,128)(2,1)}) fusion(bf16[144,5120]{1,0:T(8,128)(2,1)} %get-tuple-element.3, bf16[144,5120]{1,0:T(8,128)(2,1)} %get-tuple-element.4), kind=kLoop, calls=%fused_computation.16 | loop fusion | flops 4423680 | bytes 5898240 | tf_op jit(solution)/shard_map/broadcast_in_dim | solution.py:87
  311.3 1.1 copy.13
  312.4 0.7 convolution_convert_fusion
  313.2 1.1 copy.14
  314.3 1.2 slice_bitcast_fusion
  (22 shorter events, 0.3 us)
Async XLA Ops:
  7.2 3.8 %copy-start = (bf16[1,144,5120]{2,1,0:T(8,128)(2,1)S(1)}, bf16[1,144,5120]{2,1,0:T(8,128)(2,1)}, u32[]{:S(2)}) copy-start(bf16[1,144,5120]{2,1,0:T(8,128)(2,1)} %param.11) | copy-start | bytes 4423684
  7.2 3.8 %copy-start.1 = (bf16[1,1,18,8,5120]{4,3,2,1,0:T(8,128)(2,1)S(1)}, bf16[1,1,18,8,5120]{4,3,2,1,0:T(8,128)(2,1)}, u32[]{:S(2)}) copy-start(bf16[1,1,18,8,5120]{4,3,2,1,0:T(8,128)(2,1)} %param.9) | copy-start | bytes 4423684
  7.2 3.8 %copy-start.4 = (f32[1,5120]{1,0:T(1,128)S(1)}, f32[1,5120]{1,0:T(1,128)}, u32[]{:S(2)}) copy-start(f32[1,5120]{1,0:T(1,128)} %param.13) | copy-start | bytes 61444
  11.0 1.4 copy-start.2
  11.0 1.8 copy-start.7
  16.7 3.7 %copy-start.5 = (s32[1,1,18]{2,1,0:T(1,128)S(1)}, s32[1,1,18]{2,1,0:T(1,128)}, u32[]{:S(2)}) copy-start(s32[1,1,18]{2,1,0:T(1,128)} %param.16) | copy-start | bytes 220
  24.9 95.4 %all-to-all-start = ((bf16[24,8,5120]{2,1,0:T(8,128)(2,1)}), bf16[24,8,5120]{2,1,0:T(8,128)(2,1)}, u32[]{:S(2)}, u32[]{:S(2)}) async-start(bf16[24,8,5120]{2,1,0:T(8,128)(2,1)} %bitcast.64), calls=%async_computation | async-start | bytes 3932160 | tf_op jit(solution)/shard_map/all_to_all | solution.py:68
  41.4 265.9 %all-reduce.3.cloned.1.call-start = ((), (), s32[]{:S(2)}) async-start(), calls=%async_computation.1 | async-start | bytes 5898240 | tf_op jit(solution)/shard_map/psum | solution.py:82
  41.4 1.9 copy-start.3
  120.3 191.0 %collective-permute-start = (bf16[24,8,5120]{2,1,0:T(8,128)(2,1)}, bf16[24,8,5120]{2,1,0:T(8,128)(2,1)S(1)}, u32[]{:S(2)}, u32[]{:S(2)}) collective-permute-start(bf16[24,8,5120]{2,1,0:T(8,128)(2,1)} %all-to-all-done), channel_id=1, source_target_pairs={{24,0},{48,24},{72,48},{96,72},{120,96},{144,120},{168,144},{192,1... | collective-permute-start | bytes 5898248 | tf_op jit(solution)/shard_map/ppermute | solution.py:12
  311.3 1.1 copy-start.6
Sparse Core Ops, SparseCore 0:
  46.1 261.1 all-reduce.2
where the time goes:
time: 323 us; the launch traced here: 322 us
  waiting for transfers between devices  260 us (80%)
  starting transfers between devices  18.4 us (6%)
  between operations  14.8 us (5%)
  local copies, waits for them, and re-layouts  10.8 us (3%)
  other arithmetic  9.76 us (3%)
  matrix products  8.83 us (3%)
    psum x1, waiting for transfers between devices, on_device(): lax.psum(part_down.astype(jnp.bfloat16), 'peer').astype(jnp.float32)  184 us
    all_to_all x1, waiting for transfers between devices, on_device(): lax.all_to_all(by_sender, 'peer', split_axis=0, concat_axis=0, tiled=True)  75.3 us
    all_to_all x1, starting transfers between devices, on_device(): lax.all_to_all(by_sender, 'peer', split_axis=0, concat_axis=0, tiled=True)  16.5 us
  transfers between devices with their start and end apart: 3, of which 2 were waited for; matrix products, arithmetic and copies ran while one was open for 2% of the time, Pallas kernels for 0%

commit v1 on v0

v1 whole, which is shorter than its diff:
```python
import jax
import jax.numpy as jnp
from jax import lax
from jax.sharding import Mesh, PartitionSpec as P

epsilon = 1e-05
SECTION = ("section",)


def permuted(block, axes, route):
    return lax.ppermute(block, axes, route)


def compact(blocks, targets, live_count):
    peer_count = blocks.shape[0]
    send_slots = targets.shape[0]
    peer_index = jnp.arange(peer_count, dtype=jnp.int32)
    slot_index = jnp.arange(send_slots, dtype=jnp.int32)
    selector = (
        (targets[:, None] == peer_index[None, :]) & (slot_index[:, None] < live_count)
    ).astype(jnp.bfloat16)
    flat = blocks.reshape(peer_count, -1)
    packed = jnp.dot(selector, flat, preferred_element_type=jnp.float32).astype(jnp.bfloat16)
    return packed.reshape((send_slots,) + blocks.shape[1:])


def on_device(stash, back_in, down_proj, up_proj, gain, sent_to, sent_count, recv_from, back_live):
    peer_count = 24
    live_slots = back_live[0, 0]
    slot_mask = live_slots.astype(jnp.bfloat16)[:, None, None]
    slot_count = stash.shape[2]
    micro_rows = stash.shape[3]
    model_width = stash.shape[4]
    rank = down_proj.shape[1]
    stored = (stash[0, 0] * slot_mask).reshape(slot_count * micro_rows, model_width)
    incoming = (back_in[0, 0] * slot_mask).reshape(slot_count * micro_rows, model_width)
    section_gain = gain[0]
    down_local = down_proj[0]
    up_local = up_proj[0]
    stored_f = stored.astype(jnp.float32)
    inverse = lax.rsqrt(jnp.mean(stored_f * stored_f, axis=-1, keepdims=True) + epsilon)
    unit_rows = stored_f * inverse
    normed = (unit_rows * section_gain).astype(jnp.bfloat16)
    contract_last = (((1,), (1,)), ((), ()))
    contract_rows = (((0,), (0,)), ((), ()))
    preact = lax.dot_general(normed, down_local, contract_last, preferred_element_type=jnp.float32)
    sigmoid_pre = jax.nn.sigmoid(preact)
    activation = (preact * sigmoid_pre).astype(jnp.bfloat16)
    back_act = lax.dot_general(
        incoming, up_local, contract_last, preferred_element_type=jnp.float32
    )
    back_pre = (back_act * (sigmoid_pre * (1.0 + preact * (1.0 - sigmoid_pre)))).astype(
        jnp.bfloat16
    )
    part_down = lax.dot_general(
        back_pre, normed, contract_rows, preferred_element_type=jnp.float32
    ).astype(jnp.bfloat16)
    part_up = lax.dot_general(
        activation, incoming, contract_rows, preferred_element_type=jnp.float32
    ).astype(jnp.bfloat16)
    parts = jnp.concatenate([part_down, part_up], axis=0)
    piece = lax.psum_scatter(parts, "z", scatter_dimension=0, tiled=True)

    back_norm = jnp.dot(back_pre, down_local, preferred_element_type=jnp.float32) * section_gain
    input_grad = incoming.astype(jnp.float32) + inverse * (
        back_norm - unit_rows * jnp.mean(back_norm * unit_rows, axis=-1, keepdims=True)
    )
    input_grad = input_grad.astype(jnp.bfloat16)
    peer_index = jnp.arange(peer_count, dtype=jnp.int32)
    spreader = (
        (recv_from[0, 0][None, :] == peer_index[:, None]) & (live_slots[None, :] == 1)
    ).astype(jnp.bfloat16)
    by_sender = jnp.dot(
        spreader, input_grad.reshape(slot_count, -1), preferred_element_type=jnp.float32
    ).astype(jnp.bfloat16)
    by_sender = by_sender.reshape(peer_count, micro_rows, model_width)
    exchanged = lax.all_to_all(by_sender, ("z", "yl"), split_axis=0, concat_axis=0, tiled=True)
    back = [((i + 1) % 32, i) for i in range(32)]
    arrived = lax.ppermute(exchanged, "section", back)
    returned = compact(arrived, sent_to[0, 0], sent_count[0, 0])

    half = model_width // 2
    quarter = half // 2
    y = lax.axis_index("yl")
    other = [(0, 1), (1, 0)]
    keep = lax.dynamic_slice_in_dim(piece, y * half, half, 1)
    give = lax.dynamic_slice_in_dim(piece, (1 - y) * half, half, 1)
    got = lax.ppermute(give, "yl", other)
    total = ((keep.astype(jnp.float32) + got.astype(jnp.float32)) / peer_count).astype(jnp.bfloat16)
    mine, theirs = [], []
    for c in range(2):
        whole = lax.all_gather(total[:, c * quarter : (c + 1) * quarter], "z", axis=0, tiled=True)
        mine.append(whole)
        theirs.append(lax.ppermute(whole, "yl", other))
    low = [jnp.where(y == 0, a, b) for a, b in zip(mine, theirs)]
    high = [jnp.where(y == 0, b, a) for a, b in zip(mine, theirs)]
    grads = jnp.concatenate(low + high, axis=1)
    return (returned[None, None], grads[None, :rank], grads[None, rank:])


def solution(mesh):
    inner = Mesh(mesh.devices.reshape(32, 12, 2), ("section", "z", "yl"))
    peer = ("z", "yl")
    placed = (
        P("section", peer, None, None, None),
        P("section", peer, None, None, None),
        P("section", None, None),
        P("section", None, None),
        P("section", None),
        P("section", peer, None),
        P("section", peer),
        P("section", peer, None),
        P("section", peer, None),
    )
    return jax.shard_map(
        on_device,
        mesh=inner,
        in_specs=placed,
        out_specs=(
            P("section", peer, None, None, None),
            P("section", None, None),
            P("section", None, None),
        ),
        check_vma=False,
    )
```

time: 323 us -> 274 us (0.85)
  the two profiles are of different devices: /device:TPU:16 before, /device:TPU:15 now
where the time goes in v1:
time: 274 us; the launch traced here: 273 us
  waiting for transfers between devices  146 us (53%)
  starting transfers between devices  41.8 us (15%)
  blocking collectives  40.3 us (15%)
  between operations  15 us (5%)
  local copies, waits for them, and re-layouts  12.6 us (5%)
  other arithmetic  10.5 us (4%)
  matrix products  6.57 us (2%)
    reduce_scatter x1, waiting for transfers between devices, on_device(): piece = lax.psum_scatter(parts, 'z', scatter_dimension=0, tiled=True)  97.6 us
    ppermute x1, waiting for transfers between devices, on_device(): arrived = lax.ppermute(exchanged, 'section', back)  44.9 us
    all_gather x2, blocking collectives, on_device(): lax.all_gather(total[:, c * quarter:(c + 1) * quarter], 'z', axis=0, tile...  40.3 us
    ppermute x1, starting transfers between devices, on_device(): arrived = lax.ppermute(exchanged, 'section', back)  18.1 us
    all_to_all x1, starting transfers between devices, on_device(): lax.all_to_all(by_sender, ('z', 'yl'), split_axis=0, concat_axis=0, tiled...  16.1 us
    unnamed x21, local copies, waits for them, and re-layouts  5.73 us
    ppermute x2, starting transfers between devices, on_device(): theirs.append(lax.ppermute(whole, 'yl', other))  5.6 us
  transfers between devices with their start and end apart: 6, of which 3 were waited for; matrix products, arithmetic and copies ran while one was open for 6% of the time, Pallas kernels for 0%

profile of v1, /device:TPU:15, one launch (start us, length us, event | category | flops | bytes accessed | tf_op | source)
XLA Modules:
  0.0 272.9 jit_solution(3503917134749873962)
XLA Ops:
  8.0 1.9 fusion
  10.2 2.2 fusion.4
  15.2 1.8 pad_maximum_fusion
  17.0 1.0 multiply_reduce_fusion
  18.4 2.3 add_convert_fusion
  20.7 2.7 reshape.93
  24.0 2.4 copy.12
  26.4 16.1 %all-to-all-start = ((bf16[24,8,5120]{2,1,0:T(8,128)(2,1)}), bf16[24,8,5120]{2,1,0:T(8,128)(2,1)}, u32[]{:S(2)}, u32[]{:S(2)}) async-start(bf16[24,8,5120]{2,1,0:T(8,128)(2,1)} %bitcast.15), calls=%async_computation | async-start | bytes 3932160 | tf_op jit(solution)/shard_map/all_to_all | solution.py:77
  42.6 97.6 %reduce-scatter.2.cloned.1.call-done = bf16[24,5120]{1,0:T(8,128)(2,1)} async-done(((bf16[288,5120]{1,0:T(8,128)(2,1)}), bf16[24,5120]{1,0:T(8,128)(2,1)}) %reduce-scatter.2.cloned.1.call-update) | async-done | bytes 245776 | tf_op jit(solution)/shard_map/reduce_scatter | solution.py:62
  141.1 1.9 collective-permute-start.1
  143.0 3.7 %collective-permute-done.1 = bf16[24,2560]{1,0:T(8,128)(2,1)S(1)} collective-permute-done((bf16[24,2560]{1,0:T(8,128)(2,1)S(1)}, bf16[24,2560]{1,0:T(8,128)(2,1)S(1)}, u32[]{:S(2)}, u32[]{:S(2)}) %collective-permute-start.1) | collective-permute-done | bytes 122912 | tf_op jit(solution)/shard_map/ppermute | solution.py:88
  146.7 0.9 multiply_convert_fusion.2
  147.7 20.4 %all_gather.7 = bf16[288,1280]{1,0:T(8,128)(2,1)S(1)} all-gather(bf16[24,1280]{1,0:T(8,128)(2,1)S(1)} %get-tuple-element.10), channel_id=1, replica_groups=mesh['section'=32,'z'=12,'yl'=2] {'z'}, dimensions={0}, use_global_device_ids=true | all-gather | bytes 798720 | tf_op jit(solution)/shard_map/all_gather | solution.py:92
  168.1 2.0 collective-permute-start.3
  170.1 19.8 %all_gather.6 = bf16[288,1280]{1,0:T(8,128)(2,1)S(1)} all-gather(bf16[24,1280]{1,0:T(8,128)(2,1)S(1)} %get-tuple-element.9), channel_id=1, replica_groups=mesh['section'=32,'z'=12,'yl'=2] {'z'}, dimensions={0}, use_global_device_ids=true | all-gather | bytes 798720 | tf_op jit(solution)/shard_map/all_gather | solution.py:92
  190.0 3.6 %collective-permute-start.2 = (bf16[288,1280]{1,0:T(8,128)(2,1)S(1)}, bf16[288,1280]{1,0:T(8,128)(2,1)}, u32[]{:S(2)}, u32[]{:S(2)}) collective-permute-start(bf16[288,1280]{1,0:T(8,128)(2,1)S(1)} %all_gather.6), channel_id=1, source_target_pairs={{0,1},{1,0},{2,3},{3,2},{4,5},{5,4},{6,7},{7,6},{8,9},{9,8},{10,11... | collective-permute-start | bytes 2211848 | tf_op jit(solution)/shard_map/ppermute | solution.py:94
  194.3 18.1 %collective-permute-start = (bf16[24,8,5120]{2,1,0:T(8,128)(2,1)}, bf16[24,8,5120]{2,1,0:T(8,128)(2,1)S(1)}, u32[]{:S(2)}, u32[]{:S(2)}) collective-permute-start(bf16[24,8,5120]{2,1,0:T(8,128)(2,1)} %all-to-all-done), channel_id=1, source_target_pairs={{24,0},{48,24},{72,48},{96,72},{120,96},{144,120},{168,144},{192,1... | collective-permute-start | bytes 5898248 | tf_op jit(solution)/shard_map/ppermute | solution.py:79
  212.4 1.2 broadcast_select_fusion.2
  213.7 1.2 broadcast_select_fusion.3
  215.2 1.8 slice_bitcast_fusion.1
  217.0 44.9 %collective-permute-done = bf16[24,8,5120]{2,1,0:T(8,128)(2,1)S(1)} collective-permute-done((bf16[24,8,5120]{2,1,0:T(8,128)(2,1)}, bf16[24,8,5120]{2,1,0:T(8,128)(2,1)S(1)}, u32[]{:S(2)}, u32[]{:S(2)}) %collective-permute-start) | collective-permute-done | bytes 1966112 | tf_op jit(solution)/shard_map/ppermute | solution.py:79
  262.0 1.1 copy.13
  263.8 1.1 copy.14
  264.9 1.2 slice_bitcast_fusion
  (39 shorter events, 6.9 us)
Async XLA Ops:
  7.2 3.0 %copy-start = (bf16[1,144,5120]{2,1,0:T(8,128)(2,1)S(1)}, bf16[1,144,5120]{2,1,0:T(8,128)(2,1)}, u32[]{:S(2)}) copy-start(bf16[1,144,5120]{2,1,0:T(8,128)(2,1)} %param.11) | copy-start | bytes 4423684
  7.2 133.0 %reduce-scatter.2.cloned.1.call-start = ((), (), s32[]{:S(2)}) async-start(), calls=%async_computation.2 | async-start | bytes 3194880 | tf_op jit(solution)/shard_map/reduce_scatter | solution.py:62
  10.2 2.3 copy-start.2
  10.2 2.3 copy-start.7
  13.1 1.4 copy-start.1
  13.1 1.4 copy-start.4
  17.0 1.4 copy-start.3
  20.7 2.7 copy-start.8
  20.7 2.7 copy-start.5
  26.4 167.8 %all-to-all-start = ((bf16[24,8,5120]{2,1,0:T(8,128)(2,1)}), bf16[24,8,5120]{2,1,0:T(8,128)(2,1)}, u32[]{:S(2)}, u32[]{:S(2)}) async-start(bf16[24,8,5120]{2,1,0:T(8,128)(2,1)} %bitcast.15), calls=%async_computation | async-start | bytes 3932160 | tf_op jit(solution)/shard_map/all_to_all | solution.py:77
  141.1 5.6 %collective-permute-start.1 = (bf16[24,2560]{1,0:T(8,128)(2,1)S(1)}, bf16[24,2560]{1,0:T(8,128)(2,1)S(1)}, u32[]{:S(2)}, u32[]{:S(2)}) collective-permute-start(bf16[24,2560]{1,0:T(8,128)(2,1)S(1)} %constant_dynamic-slice_fusion), channel_id=1, source_target_pairs={{0,1},{1,0},{2,3},{3,2},{4,5},{5,4},{6,7},{7,6},{8,9},{9,8},{10,11... | collective-permute-start | bytes 368648 | tf_op jit(solution)/shard_map/ppermute | solution.py:88
  168.1 44.3 %collective-permute-start.3 = (bf16[288,1280]{1,0:T(8,128)(2,1)S(1)}, bf16[288,1280]{1,0:T(8,128)(2,1)}, u32[]{:S(2)}, u32[]{:S(2)}) collective-permute-start(bf16[288,1280]{1,0:T(8,128)(2,1)S(1)} %all_gather.7), channel_id=1, source_target_pairs={{0,1},{1,0},{2,3},{3,2},{4,5},{5,4},{6,7},{7,6},{8,9},{9,8},{10,11... | collective-permute-start | bytes 2211848 | tf_op jit(solution)/shard_map/ppermute | solution.py:94
  190.0 23.7 %collective-permute-start.2 = (bf16[288,1280]{1,0:T(8,128)(2,1)S(1)}, bf16[288,1280]{1,0:T(8,128)(2,1)}, u32[]{:S(2)}, u32[]{:S(2)}) collective-permute-start(bf16[288,1280]{1,0:T(8,128)(2,1)S(1)} %all_gather.6), channel_id=1, source_target_pairs={{0,1},{1,0},{2,3},{3,2},{4,5},{5,4},{6,7},{7,6},{8,9},{9,8},{10,11... | collective-permute-start | bytes 2211848 | tf_op jit(solution)/shard_map/ppermute | solution.py:94
  194.3 67.7 %collective-permute-start = (bf16[24,8,5120]{2,1,0:T(8,128)(2,1)}, bf16[24,8,5120]{2,1,0:T(8,128)(2,1)S(1)}, u32[]{:S(2)}, u32[]{:S(2)}) collective-permute-start(bf16[24,8,5120]{2,1,0:T(8,128)(2,1)} %all-to-all-done), channel_id=1, source_target_pairs={{24,0},{48,24},{72,48},{96,72},{120,96},{144,120},{168,144},{192,1... | collective-permute-start | bytes 5898248 | tf_op jit(solution)/shard_map/ppermute | solution.py:79
  262.0 1.1 copy-start.6
Sparse Core Ops, SparseCore 0:
  17.2 123.0 reduce-scatter.1

commit v2 on v1

v2 whole, which is shorter than its diff:
```python
import jax
import jax.numpy as jnp
from jax import lax
from jax.experimental import pallas as pl
from jax.experimental.pallas import tpu as pltpu
from jax.sharding import Mesh, PartitionSpec as P

epsilon = 1e-05
SECTIONS, Z, Y = 32, 12, 2
PEERS = Z * Y
SLOTS, MB, D, RANK = 18, 8, 5120, 144
ROWS = SLOTS * MB
HALF = D // 2
CHUNK = 512
WIDE = 1792
NARROW = HALF - WIDE
LAST = (((1,), (1,)), ((), ()))
FIRST = (((0,), (0,)), ((), ()))
VMEM_LIMIT = 60 * 2**20


def _chunks(width, step):
    return [slice(c, c + step) for c in range(0, width, step)]


def _local(
    y_ref, recv_ref, live_ref, gain, stash_hbm, back_in_hbm, down_hbm, up_hbm,
    out_hbm, give_hbm, keep_hbm,
    stash, back_in, down, up, mask, normed, out, give, keep, sems,
):
    f32, bf16 = jnp.float32, jnp.bfloat16
    pairs = ((stash_hbm, stash), (down_hbm, down), (back_in_hbm, back_in), (up_hbm, up))
    loads = [pltpu.make_async_copy(a, b, sems.at[i]) for i, (a, b) in enumerate(pairs)]
    for load in loads:
        load.start()
    for slot in range(SLOTS):
        mask[MB * slot : MB * (slot + 1), :] = jnp.full((MB, 128), live_ref[slot].astype(f32), f32)
    for peer in range(PEERS):
        out[peer] = jnp.zeros((MB, D), bf16)
    loads[0].wait()
    squares = jnp.zeros((ROWS, 128), f32)
    for cols in _chunks(D, 128):
        s = stash[:, cols].astype(f32)
        squares += s * s
    live = mask[:, :1]
    inverse = lax.rsqrt(jnp.sum(squares, axis=1, keepdims=True) * (1.0 / D) + epsilon) * live
    for load in loads[1:]:
        load.wait()
    preact = jnp.zeros((ROWS, RANK), f32)
    back_act = jnp.zeros((ROWS, RANK), f32)
    for cols in _chunks(D, CHUNK):
        n = (stash[:, cols].astype(f32) * inverse * gain[:, cols]).astype(bf16)
        normed[:, cols] = n
        preact += lax.dot_general(n, down[:, cols], LAST, preferred_element_type=f32)
        back_act += lax.dot_general(back_in[:, cols], up[:, cols], LAST, preferred_element_type=f32)
    sigmoid = 1.0 / (1.0 + jnp.exp(-preact))
    act = (preact * sigmoid).astype(bf16)
    pre = (back_act * live * (sigmoid * (1.0 + preact * (1.0 - sigmoid)))).astype(bf16)
    shared = jnp.sum(pre.astype(f32) * preact, axis=1, keepdims=True) * (inverse * (1.0 / D))
    alive = live > 0.5
    for cols in _chunks(D, CHUNK):
        back_norm = jnp.dot(pre, down[:, cols], preferred_element_type=f32) * gain[:, cols]
        unit = stash[:, cols].astype(f32) * inverse
        grad = back_in[:, cols].astype(f32) + inverse * back_norm - unit * shared
        grad = jnp.where(alive, grad, 0.0)
        for slot in range(SLOTS):
            out[recv_ref[slot], :, cols] = grad[MB * slot : MB * (slot + 1), :].astype(bf16)
    stores = [pltpu.make_async_copy(out, out_hbm, sems.at[4])]
    stores[0].start()
    y = y_ref[0]
    for place, target, half in ((give, give_hbm, 1 - y), (keep, keep_hbm, y)):
        for cols in _chunks(HALF, CHUNK):
            here = pl.ds(pl.multiple_of(half * HALF + cols.start, 128), CHUNK)
            place[:RANK, cols] = lax.dot_general(
                pre, normed[:, here], FIRST, preferred_element_type=f32
            ).astype(bf16)
            place[RANK:, cols] = lax.dot_general(
                act, back_in[:, here], FIRST, preferred_element_type=f32
            ).astype(bf16)
        stores.append(pltpu.make_async_copy(place, target, sems.at[4 + len(stores)]))
        stores[-1].start()
    for store in stores:
        store.wait()


def local(y, recv, live, gain, stash, back_in, down, up):
    smem = pl.BlockSpec(memory_space=pltpu.SMEM)
    vmem = pl.BlockSpec(memory_space=pltpu.VMEM)
    hbm = pl.BlockSpec(memory_space=pl.ANY)
    bf16 = jnp.bfloat16
    outs = ((PEERS, MB, D), (2 * RANK, HALF), (2 * RANK, HALF))
    return pl.pallas_call(
        _local,
        out_shape=tuple(jax.ShapeDtypeStruct(shape, bf16) for shape in outs),
        in_specs=[smem, smem, smem, vmem] + [hbm] * 4,
        out_specs=[hbm] * 3,
        scratch_shapes=[
            pltpu.VMEM((ROWS, D), bf16),
            pltpu.VMEM((ROWS, D), bf16),
            pltpu.VMEM((RANK, D), bf16),
            pltpu.VMEM((RANK, D), bf16),
            pltpu.VMEM((ROWS, 128), jnp.float32),
            pltpu.VMEM((ROWS, D), bf16),
        ]
        + [pltpu.VMEM(shape, bf16) for shape in outs]
        + [pltpu.SemaphoreType.DMA((7,))],
        compiler_params=pltpu.CompilerParams(vmem_limit_bytes=VMEM_LIMIT),
        cost_estimate=pl.CostEstimate(
            flops=10 * ROWS * RANK * D, bytes_accessed=16 * ROWS * D, transcendentals=ROWS * RANK
        ),
        name="local",
    )(y, recv, live, gain, stash, back_in, down, up)


def _compact(wiring, blocks, out, sems):
    for slot in range(SLOTS):

        @pl.when(slot < wiring[SLOTS])
        def _(slot=slot):
            pltpu.make_async_copy(blocks.at[wiring[slot]], out.at[slot], sems.at[slot]).start()

    for slot in range(SLOTS):
        live = slot < wiring[SLOTS]

        @pl.when(jnp.logical_not(live))
        def _(slot=slot):
            out[slot] = jnp.zeros((MB, D), jnp.bfloat16)

        @pl.when(live)
        def _(slot=slot):
            pltpu.make_async_copy(blocks.at[wiring[slot]], out.at[slot], sems.at[slot]).wait()


def compact(wiring, blocks):
    return pl.pallas_call(
        _compact,
        out_shape=jax.ShapeDtypeStruct((SLOTS, MB, D), jnp.bfloat16),
        in_specs=[pl.BlockSpec(memory_space=pltpu.SMEM), pl.BlockSpec(memory_space=pl.ANY)],
        out_specs=pl.BlockSpec(memory_space=pltpu.VMEM),
        scratch_shapes=[pltpu.SemaphoreType.DMA((SLOTS,))],
        compiler_params=pltpu.CompilerParams(vmem_limit_bytes=VMEM_LIMIT),
        cost_estimate=pl.CostEstimate(flops=0, bytes_accessed=5 * ROWS * D, transcendentals=0),
        name="compact",
    )(wiring, blocks)


def on_device(stash, back_in, down_proj, up_proj, gain, sent_to, sent_count, recv_from, back_live):
    f32, bf16 = jnp.float32, jnp.bfloat16
    y = lax.axis_index("yl")
    swap = [(0, 1), (1, 0)]
    back = [((i + 1) % SECTIONS, i) for i in range(SECTIONS)]
    ahead = [(i, (i + 1) % SECTIONS) for i in range(SECTIONS)]
    stash = stash.reshape(ROWS, D)
    back_in = back_in.reshape(ROWS, D)
    live, recv = back_live[0, 0], recv_from[0, 0]
    by_sender, give, keep = local(
        y.astype(jnp.int32).reshape(1), recv, live, gain, stash, back_in, down_proj[0], up_proj[0]
    )
    exchanged = lax.all_to_all(by_sender, ("z", "yl"), split_axis=0, concat_axis=0, tiled=True)
    got = lax.ppermute(give, "yl", swap)
    wiring = lax.ppermute(jnp.concatenate([sent_to[0, 0], sent_count[0]]), "section", ahead)
    keep, wiring = lax.optimization_barrier((keep, wiring))
    pair = (keep.astype(f32) + got.astype(f32)).astype(bf16)
    shard = lax.psum_scatter(pair.reshape(180, 4096), "z", scatter_dimension=0, tiled=True)
    mean = (shard.astype(f32) / PEERS).astype(bf16).reshape(24, HALF)
    wide, narrow = mean[:, :WIDE], mean[:, WIDE:]
    narrow_got = lax.ppermute(narrow, "yl", swap)
    narrow_both = jnp.concatenate(
        [jnp.where(y == 0, narrow, narrow_got), jnp.where(y == 0, narrow_got, narrow)], axis=1
    )
    wide, exchanged = lax.optimization_barrier((wide, exchanged))
    packed = compact(wiring, exchanged)
    returned = lax.ppermute(packed, "section", back)
    wide_mine = lax.all_gather(wide, "z", axis=0, tiled=True)
    wide_got = lax.ppermute(wide_mine, "yl", swap)
    narrow_both, wide_mine, returned = lax.optimization_barrier((narrow_both, wide_mine, returned))
    narrow_all = lax.all_gather(narrow_both, "z", axis=0, tiled=True)
    grads = jnp.concatenate(
        [
            jnp.where(y == 0, wide_mine, wide_got),
            narrow_all[:, :NARROW],
            jnp.where(y == 0, wide_got, wide_mine),
            narrow_all[:, NARROW:],
        ],
        axis=1,
    )
    return (
        returned.reshape(1, 1, SLOTS, MB, D),
        grads[None, :RANK],
        grads[None, RANK:],
    )


def solution(mesh):
    inner = Mesh(mesh.devices.reshape(SECTIONS, Z, Y), ("section", "z", "yl"))
    peer = ("z", "yl")
    placed = (
        P("section", peer, None, None, None),
        P("section", peer, None, None, None),
        P("section", None, None),
        P("section", None, None),
        P("section", None),
        P("section", peer, None),
        P("section", peer),
        P("section", peer, None),
        P("section", peer, None),
    )
    return jax.shard_map(
        on_device,
        mesh=inner,
        in_specs=placed,
        out_specs=(
            P("section", peer, None, None, None),
            P("section", None, None),
            P("section", None, None),
        ),
        check_vma=False,
    )
```

time: 274 us -> 205 us (0.75)
  the two profiles are of different devices: /device:TPU:15 before, /device:TPU:16 now
where the time goes in v2:
time: 205 us; the launch traced here: 204 us
  blocking collectives  96.9 us (47%)
  waiting for transfers between devices  47.1 us (23%)
  starting transfers between devices  32.8 us (16%)
  local copies, waits for them, and re-layouts  11.6 us (6%)
  Pallas kernels  11.5 us (6%)
  other arithmetic  2.18 us (1%)
  between operations  2.15 us (1%)
    ppermute x1, waiting for transfers between devices, on_device(): lax.ppermute(jnp.concatenate([sent_to[0, 0], sent_count[0]]), 'section',...  43 us
    unnamed x1, blocking collectives  37.2 us
    all_gather x1, blocking collectives, on_device(): narrow_all = lax.all_gather(narrow_both, 'z', axis=0, tiled=True)  30.2 us
    all_gather x1, blocking collectives, on_device(): wide_mine = lax.all_gather(wide, 'z', axis=0, tiled=True)  29.6 us
    all_to_all x1, starting transfers between devices, on_device(): lax.all_to_all(by_sender, ('z', 'yl'), split_axis=0, concat_axis=0, tiled...  16.5 us
    pallas_call x1, Pallas kernels, local(): pl.pallas_call(_local, out_shape=tuple((jax.ShapeDtypeStruct(shape, bf16)...  8.17 us
    unnamed x12, local copies, waits for them, and re-layouts  6.5 us
  transfers between devices with their start and end apart: 7, of which 4 were waited for; matrix products, arithmetic and copies ran while one was open for 23% of the time, Pallas kernels for 0%

profile of v2, /device:TPU:16, one launch (start us, length us, event | category | flops | bytes accessed | tf_op | source)
XLA Modules:
  0.0 204.3 jit_solution(15396454849155044674)
XLA Ops:
  0.6 8.2 %local.1 = (bf16[24,8,5120]{2,1,0:T(8,128)(2,1)}, bf16[288,2560]{1,0:T(8,128)(2,1)}, bf16[288,2560]{1,0:T(8,128)(2,1)}) custom-call(s32[1]{0:T(128)} %bitcast.y_ref, s32[18]{0:T(128)} %bitcast.23, s32[18]{0:T(128)} %bitcast.24, f32[1,5120]{1,0:T(1,128)} %gain.1, bf16[144,5120]{1,0:T(8,128)(2,1)} %bitcast.18, bf16[144,5120]{1,0:T(8,128)(2,1)} %bitcast.19, ...), custom_call_target="tpu_custom_call" | custom-call | flops 1061683200 | bytes 11796480 | tf_op jit(solution)/shard_map/local/pallas_call | solution.py:92
  8.8 16.5 %all-to-all-start = ((bf16[24,8,5120]{2,1,0:T(8,128)(2,1)}), bf16[24,8,5120]{2,1,0:T(8,128)(2,1)S(1)}, u32[]{:S(2)}, u32[]{:S(2)}) async-start(bf16[24,8,5120]{2,1,0:T(8,128)(2,1)} %get-tuple-element.16), calls=%async_computation | async-start | bytes 3932160 | tf_op jit(solution)/shard_map/all_to_all | solution.py:159
  25.4 3.8 %collective-permute-start.1 = (bf16[288,2560]{1,0:T(8,128)(2,1)}, bf16[288,2560]{1,0:T(8,128)(2,1)S(1)}, u32[]{:S(2)}, u32[]{:S(2)}) collective-permute-start(bf16[288,2560]{1,0:T(8,128)(2,1)} %get-tuple-element.15), channel_id=1, source_target_pairs={{0,1},{1,0},{2,3},{3,2},{4,5},{5,4},{6,7},{7,6},{8,9},{9,8},{10,11... | collective-permute-start | bytes 4423688 | tf_op jit(solution)/shard_map/ppermute | solution.py:160
  29.9 1.9 collective-permute-start
  31.8 43.0 %collective-permute-done.wiring = s32[19]{0:T(128)S(1)} collective-permute-done((s32[19]{0:T(128)S(1)}, s32[19]{0:T(128)S(1)}, u32[]{:S(2)}, u32[]{:S(2)}) %collective-permute-start) | collective-permute-done | bytes 108 | tf_op jit(solution)/shard_map/ppermute | solution.py:161
  75.0 1.5 add_convert_fusion
  76.5 3.1 %reshape.27 = bf16[180,4096]{1,0:T(8,128)(2,1)S(1)} reshape(bf16[288,2560]{1,0:T(8,128)(2,1)} %add_convert_fusion) | data formatting | bytes 2949120 | tf_op jit(solution)/shard_map/reshape | solution.py:164
  79.6 37.2 %fusion = bf16[16,4096]{1,0:T(8,128)(2,1)} fusion(bf16[180,4096]{1,0:T(8,128)(2,1)S(1)} %reshape.27), kind=kCustom, calls=%all-reduce-scatter | all-reduce-scatter fusion | flops 786433 | bytes 1609728
  116.8 0.9 slice.30
  117.7 2.9 %collective-permute-start.5 = (bf16[11,4096]{1,0:T(8,128)(2,1)S(1)}, bf16[11,4096]{1,0:T(8,128)(2,1)S(1)}, u32[]{:S(2)}, u32[]{:S(2)}) collective-permute-start(bf16[11,4096]{1,0:T(8,128)(2,1)S(1)} %slice.30), channel_id=1, source_target_pairs={{0,2},{2,4},{4,6},{6,8},{8,10},{10,12},{12,14},{14,16},{16,18},{18... | collective-permute-start | bytes 270344
  120.7 1.3 dynamic-slice.4
  122.6 0.6 collective-permute-done.5
  123.2 1.9 concatenate.12
  125.3 1.3 copy-done
  126.6 3.3 %compact.1 = bf16[18,8,5120]{2,1,0:T(8,128)(2,1)} custom-call(s32[19]{0:T(128)} %copy-done.2, bf16[24,8,5120]{2,1,0:T(8,128)(2,1)} %copy-done), custom_call_target="tpu_custom_call" | custom-call | bytes 3686400 | tf_op jit(solution)/shard_map/compact/pallas_call | solution.py:135
  130.0 1.9 collective-permute-start.3
  131.9 3.5 %collective-permute-start.2 = (bf16[24,768]{1,0:T(8,128)(2,1)S(1)}, bf16[24,768]{1,0:T(8,128)(2,1)S(1)}, u32[]{:S(2)}, u32[]{:S(2)}) collective-permute-start(bf16[24,768]{1,0:T(8,128)(2,1)S(1)} %slice.24), channel_id=1, source_target_pairs={{0,1},{1,0},{2,3},{3,2},{4,5},{5,4},{6,7},{7,6},{8,9},{9,8},{10,11... | collective-permute-start | bytes 110600 | tf_op jit(solution)/shard_map/ppermute | solution.py:167
  135.4 29.6 %all_gather.6 = bf16[288,1792]{1,0:T(8,128)(2,1)S(1)} all-gather(bf16[24,1792]{1,0:T(8,128)(2,1)S(1)} %slice.25), channel_id=1, replica_groups=mesh['section'=32,'z'=12,'yl'=2] {'z'}, dimensions={0}, use_global_device_ids=true | all-gather | bytes 1118208 | tf_op jit(solution)/shard_map/all_gather | solution.py:174
  164.9 2.3 %collective-permute-start.4 = (bf16[288,1792]{1,0:T(8,128)(2,1)S(1)}, bf16[288,1792]{1,0:T(8,128)(2,1)S(1)}, u32[]{:S(2)}, u32[]{:S(2)}) collective-permute-start(bf16[288,1792]{1,0:T(8,128)(2,1)S(1)} %all_gather.6), channel_id=1, source_target_pairs={{0,1},{1,0},{2,3},{3,2},{4,5},{5,4},{6,7},{7,6},{8,9},{9,8},{10,11... | collective-permute-start | bytes 3096584 | tf_op jit(solution)/shard_map/ppermute | solution.py:175
  167.3 3.4 %collective-permute-done.2 = bf16[24,768]{1,0:T(8,128)(2,1)S(1)} collective-permute-done((bf16[24,768]{1,0:T(8,128)(2,1)S(1)}, bf16[24,768]{1,0:T(8,128)(2,1)S(1)}, u32[]{:S(2)}, u32[]{:S(2)}) %collective-permute-start.2) | collective-permute-done | bytes 36896 | tf_op jit(solution)/shard_map/ppermute | solution.py:167
  170.7 30.2 %all_gather.7 = bf16[288,1536]{1,0:T(8,128)(2,1)S(1)} all-gather(bf16[24,1536]{1,0:T(8,128)(2,1)S(1)} %pad_maximum_fusion.1), channel_id=1, replica_groups=mesh['section'=32,'z'=12,'yl'=2] {'z'}, dimensions={0}, use_global_device_ids=true | all-gather | bytes 958464 | tf_op jit(solution)/shard_map/all_gather | solution.py:177
  201.1 0.4 pad_maximum_fusion
  201.4 1.8 slice_bitcast_fusion
  203.2 1.1 copy.14
  (20 shorter events, 0.8 us)
Async XLA Ops:
  8.8 21.0 %copy-start.3 = (s32[1,1,18]{2,1,0:T(1,128)S(1)}, s32[1,1,18]{2,1,0:T(1,128)}, u32[]{:S(2)}) copy-start(s32[1,1,18]{2,1,0:T(1,128)} %param.14) | copy-start | bytes 220
  8.8 66.2 %copy-start.1 = (bf16[288,2560]{1,0:T(8,128)(2,1)S(1)}, bf16[288,2560]{1,0:T(8,128)(2,1)}, u32[]{:S(2)}) copy-start(bf16[288,2560]{1,0:T(8,128)(2,1)} %get-tuple-element.14) | copy-start | bytes 4423684
  8.8 116.5 %all-to-all-start = ((bf16[24,8,5120]{2,1,0:T(8,128)(2,1)}), bf16[24,8,5120]{2,1,0:T(8,128)(2,1)S(1)}, u32[]{:S(2)}, u32[]{:S(2)}) async-start(bf16[24,8,5120]{2,1,0:T(8,128)(2,1)} %get-tuple-element.16), calls=%async_computation | async-start | bytes 3932160 | tf_op jit(solution)/shard_map/all_to_all | solution.py:159
  25.4 49.6 %collective-permute-start.1 = (bf16[288,2560]{1,0:T(8,128)(2,1)}, bf16[288,2560]{1,0:T(8,128)(2,1)S(1)}, u32[]{:S(2)}, u32[]{:S(2)}) collective-permute-start(bf16[288,2560]{1,0:T(8,128)(2,1)} %get-tuple-element.15), channel_id=1, source_target_pairs={{0,1},{1,0},{2,3},{3,2},{4,5},{5,4},{6,7},{7,6},{8,9},{9,8},{10,11... | collective-permute-start | bytes 4423688 | tf_op jit(solution)/shard_map/ppermute | solution.py:160
  29.9 44.9 %collective-permute-start = (s32[19]{0:T(128)S(1)}, s32[19]{0:T(128)S(1)}, u32[]{:S(2)}, u32[]{:S(2)}) collective-permute-start(s32[19]{0:T(128)S(1)} %pad_add_fusion), channel_id=1, source_target_pairs={{0,24},{24,48},{48,72},{72,96},{96,120},{120,144},{144,168},{168,1... | collective-permute-start | bytes 236 | tf_op jit(solution)/shard_map/ppermute | solution.py:161
  74.8 1.8 copy-start.2
  117.7 5.4 %collective-permute-start.5 = (bf16[11,4096]{1,0:T(8,128)(2,1)S(1)}, bf16[11,4096]{1,0:T(8,128)(2,1)S(1)}, u32[]{:S(2)}, u32[]{:S(2)}) collective-permute-start(bf16[11,4096]{1,0:T(8,128)(2,1)S(1)} %slice.30), channel_id=1, source_target_pairs={{0,2},{2,4},{4,6},{6,8},{8,10},{10,12},{12,14},{14,16},{16,18},{18... | collective-permute-start | bytes 270344
  125.3 1.3 copy-start
  130.0 40.7 %collective-permute-start.3 = (bf16[18,8,5120]{2,1,0:T(8,128)(2,1)}, bf16[18,8,5120]{2,1,0:T(8,128)(2,1)S(1)}, u32[]{:S(2)}, u32[]{:S(2)}) collective-permute-start(bf16[18,8,5120]{2,1,0:T(8,128)(2,1)} %compact.1), channel_id=1, source_target_pairs={{24,0},{48,24},{72,48},{96,72},{120,96},{144,120},{168,144},{192,1... | collective-permute-start | bytes 4423688 | tf_op jit(solution)/shard_map/ppermute | solution.py:173
  131.9 38.7 %collective-permute-start.2 = (bf16[24,768]{1,0:T(8,128)(2,1)S(1)}, bf16[24,768]{1,0:T(8,128)(2,1)S(1)}, u32[]{:S(2)}, u32[]{:S(2)}) collective-permute-start(bf16[24,768]{1,0:T(8,128)(2,1)S(1)} %slice.24), channel_id=1, source_target_pairs={{0,1},{1,0},{2,3},{3,2},{4,5},{5,4},{6,7},{7,6},{8,9},{9,8},{10,11... | collective-permute-start | bytes 110600 | tf_op jit(solution)/shard_map/ppermute | solution.py:167
  164.9 36.0 %collective-permute-start.4 = (bf16[288,1792]{1,0:T(8,128)(2,1)S(1)}, bf16[288,1792]{1,0:T(8,128)(2,1)S(1)}, u32[]{:S(2)}, u32[]{:S(2)}) collective-permute-start(bf16[288,1792]{1,0:T(8,128)(2,1)S(1)} %all_gather.6), channel_id=1, source_target_pairs={{0,1},{1,0},{2,3},{3,2},{4,5},{5,4},{6,7},{7,6},{8,9},{9,8},{10,11... | collective-permute-start | bytes 3096584 | tf_op jit(solution)/shard_map/ppermute | solution.py:175

commit v3 on v2

--- a/solution.py
+++ b/solution.py
@@ -138,7 +138,7 @@
         in_specs=[pl.BlockSpec(memory_space=pltpu.SMEM), pl.BlockSpec(memory_space=pl.ANY)],
         out_specs=pl.BlockSpec(memory_space=pltpu.VMEM),
         scratch_shapes=[pltpu.SemaphoreType.DMA((SLOTS,))],
-        compiler_params=pltpu.CompilerParams(vmem_limit_bytes=VMEM_LIMIT),
+        compiler_params=pltpu.CompilerParams(vmem_limit_bytes=8 * 2**20),
         cost_estimate=pl.CostEstimate(flops=0, bytes_accessed=5 * ROWS * D, transcendentals=0),
         name="compact",
     )(wiring, blocks)
@@ -160,20 +160,21 @@
     got = lax.ppermute(give, "yl", swap)
     wiring = lax.ppermute(jnp.concatenate([sent_to[0, 0], sent_count[0]]), "section", ahead)
     keep, wiring = lax.optimization_barrier((keep, wiring))
+    packed = compact(wiring, exchanged)
+    returned = lax.ppermute(packed, "section", back)
     pair = (keep.astype(f32) + got.astype(f32)).astype(bf16)
-    shard = lax.psum_scatter(pair.reshape(180, 4096), "z", scatter_dimension=0, tiled=True)
+    pair, packed = lax.optimization_barrier((pair.reshape(180, 4096), packed))
+    shard = lax.psum_scatter(pair, "z", scatter_dimension=0, tiled=True)
     mean = (shard.astype(f32) / PEERS).astype(bf16).reshape(24, HALF)
     wide, narrow = mean[:, :WIDE], mean[:, WIDE:]
     narrow_got = lax.ppermute(narrow, "yl", swap)
     narrow_both = jnp.concatenate(
         [jnp.where(y == 0, narrow, narrow_got), jnp.where(y == 0, narrow_got, narrow)], axis=1
     )
-    wide, exchanged = lax.optimization_barrier((wide, exchanged))
-    packed = compact(wiring, exchanged)
-    returned = lax.ppermute(packed, "section", back)
+    wide, returned = lax.optimization_barrier((wide, returned))
     wide_mine = lax.all_gather(wide, "z", axis=0, tiled=True)
     wide_got = lax.ppermute(wide_mine, "yl", swap)
-    narrow_both, wide_mine, returned = lax.optimization_barrier((narrow_both, wide_mine, returned))
+    narrow_both, wide_mine = lax.optimization_barrier((narrow_both, wide_mine))
     narrow_all = lax.all_gather(narrow_both, "z", axis=0, tiled=True)
     grads = jnp.concatenate(
         [

time: 205 us -> 206 us (level)
  the two profiles are of different devices: /device:TPU:16 before, /device:TPU:64 now
where the time goes in v3:
time: 206 us; the launch traced here: 205 us
  blocking collectives  87.8 us (43%)
  waiting for transfers between devices  58.7 us (28%)
  starting transfers between devices  35.3 us (17%)
  Pallas kernels  11 us (5%)
  local copies, waits for them, and re-layouts  7.62 us (4%)
  other arithmetic  2.43 us (1%)
  between operations  2.16 us (1%)
    ppermute x1, waiting for transfers between devices, on_device(): lax.ppermute(jnp.concatenate([sent_to[0, 0], sent_count[0]]), 'section',...  44.9 us
    unnamed x1, blocking collectives  34.7 us
    all_gather x1, blocking collectives, on_device(): narrow_all = lax.all_gather(narrow_both, 'z', axis=0, tiled=True)  26.6 us
    all_gather x1, blocking collectives, on_device(): wide_mine = lax.all_gather(wide, 'z', axis=0, tiled=True)  26.5 us
    all_to_all x1, starting transfers between devices, on_device(): lax.all_to_all(by_sender, ('z', 'yl'), split_axis=0, concat_axis=0, tiled...  16 us
    all_to_all x1, waiting for transfers between devices, on_device(): lax.all_to_all(by_sender, ('z', 'yl'), split_axis=0, concat_axis=0, tiled...  11.2 us
    pallas_call x1, Pallas kernels, local(): pl.pallas_call(_local, out_shape=tuple((jax.ShapeDtypeStruct(shape, bf16)...  8.16 us
    ppermute x1, starting transfers between devices, on_device(): wide_got = lax.ppermute(wide_mine, 'yl', swap)  4.84 us
  transfers between devices with their start and end apart: 7, of which 3 were waited for; matrix products, arithmetic and copies ran while one was open for 20% of the time, Pallas kernels for 0%

profile of v3, /device:TPU:64, one launch (start us, length us, event | category | flops | bytes accessed | tf_op | source)
XLA Modules:
  0.0 205.0 jit_solution(3249845801268935696)
XLA Ops:
  0.6 8.2 %local.1 = (bf16[24,8,5120]{2,1,0:T(8,128)(2,1)}, bf16[288,2560]{1,0:T(8,128)(2,1)}, bf16[288,2560]{1,0:T(8,128)(2,1)}) custom-call(s32[1]{0:T(128)} %bitcast.y_ref, s32[18]{0:T(128)} %bitcast.23, s32[18]{0:T(128)} %bitcast.24, f32[1,5120]{1,0:T(1,128)} %gain.1, bf16[144,5120]{1,0:T(8,128)(2,1)} %bitcast.18, bf16[144,5120]{1,0:T(8,128)(2,1)} %bitcast.19, ...), custom_call_target="tpu_custom_call" | custom-call | flops 1061683200 | bytes 11796480 | tf_op jit(solution)/shard_map/local/pallas_call | solution.py:92
  8.8 16.0 %all-to-all-start = ((bf16[24,8,5120]{2,1,0:T(8,128)(2,1)}), bf16[24,8,5120]{2,1,0:T(8,128)(2,1)S(1)}, u32[]{:S(2)}, u32[]{:S(2)}) async-start(bf16[24,8,5120]{2,1,0:T(8,128)(2,1)} %get-tuple-element.17), calls=%async_computation | async-start | bytes 3932160 | tf_op jit(solution)/shard_map/all_to_all | solution.py:159
  24.8 3.4 %collective-permute-start.1 = (bf16[288,2560]{1,0:T(8,128)(2,1)S(1)}, bf16[288,2560]{1,0:T(8,128)(2,1)S(1)}, u32[]{:S(2)}, u32[]{:S(2)}) collective-permute-start(bf16[288,2560]{1,0:T(8,128)(2,1)S(1)} %copy-done), channel_id=1, source_target_pairs={{0,1},{1,0},{2,3},{3,2},{4,5},{5,4},{6,7},{7,6},{8,9},{9,8},{10,11... | collective-permute-start | bytes 4423688 | tf_op jit(solution)/shard_map/ppermute | solution.py:160
  29.0 1.9 collective-permute-start
  30.9 44.9 %collective-permute-done.wiring = s32[19]{0:T(128)S(1)} collective-permute-done((s32[19]{0:T(128)S(1)}, s32[19]{0:T(128)S(1)}, u32[]{:S(2)}, u32[]{:S(2)}) %collective-permute-start) | collective-permute-done | bytes 108 | tf_op jit(solution)/shard_map/ppermute | solution.py:161
  75.8 1.8 add_convert_fusion
  77.6 2.9 %reshape.27 = bf16[180,4096]{1,0:T(8,128)(2,1)} reshape(bf16[288,2560]{1,0:T(8,128)(2,1)S(1)} %add_convert_fusion) | data formatting | bytes 2949120 | tf_op jit(solution)/shard_map/reshape | solution.py:166
  80.5 11.2 %all-to-all-done.blocks = bf16[24,8,5120]{2,1,0:T(8,128)(2,1)S(1)} async-done(((bf16[24,8,5120]{2,1,0:T(8,128)(2,1)}), bf16[24,8,5120]{2,1,0:T(8,128)(2,1)S(1)}, u32[]{:S(2)}, u32[]{:S(2)}) %all-to-all-start) | async-done | bytes 1966112 | tf_op jit(solution)/shard_map/all_to_all | solution.py:159
  91.7 2.8 %compact.1 = bf16[18,8,5120]{2,1,0:T(8,128)(2,1)S(1)} custom-call(s32[19]{0:T(128)S(1)} %collective-permute-done.wiring, bf16[24,8,5120]{2,1,0:T(8,128)(2,1)S(1)} %all-to-all-done.blocks), custom_call_target="tpu_custom_call" | custom-call | bytes 3686400 | tf_op jit(solution)/shard_map/compact/pallas_call | solution.py:135
  94.5 4.2 %collective-permute-start.2 = (bf16[18,8,5120]{2,1,0:T(8,128)(2,1)S(1)}, bf16[18,8,5120]{2,1,0:T(8,128)(2,1)S(1)}, u32[]{:S(2)}, u32[]{:S(2)}) collective-permute-start(bf16[18,8,5120]{2,1,0:T(8,128)(2,1)S(1)} %compact.1), channel_id=1, source_target_pairs={{24,0},{48,24},{72,48},{96,72},{120,96},{144,120},{168,144},{192,1... | collective-permute-start | bytes 4423688 | tf_op jit(solution)/shard_map/ppermute | solution.py:164
  98.7 34.7 %fusion = bf16[16,4096]{1,0:T(8,128)(2,1)S(1)} fusion(bf16[180,4096]{1,0:T(8,128)(2,1)} %reshape.27), kind=kCustom, calls=%all-reduce-scatter | all-reduce-scatter fusion | flops 786433 | bytes 1609728
  133.5 3.0 %collective-permute-start.5 = (bf16[11,4096]{1,0:T(8,128)(2,1)S(1)}, bf16[11,4096]{1,0:T(8,128)(2,1)S(1)}, u32[]{:S(2)}, u32[]{:S(2)}) collective-permute-start(bf16[11,4096]{1,0:T(8,128)(2,1)S(1)} %slice.30), channel_id=1, source_target_pairs={{0,2},{2,4},{4,6},{6,8},{8,10},{10,12},{12,14},{14,16},{16,18},{18... | collective-permute-start | bytes 270344
  136.5 1.3 dynamic-slice.4
  138.5 2.5 %collective-permute-done.5 = bf16[11,4096]{1,0:T(8,128)(2,1)S(1)} collective-permute-done((bf16[11,4096]{1,0:T(8,128)(2,1)S(1)}, bf16[11,4096]{1,0:T(8,128)(2,1)S(1)}, u32[]{:S(2)}, u32[]{:S(2)}) %collective-permute-start.5) | collective-permute-done | bytes 90144
  141.0 0.3 concatenate.12
  141.4 0.2 reshape.28
  141.6 1.9 collective-permute-start.3
  143.5 26.5 %all_gather.6 = bf16[288,1792]{1,0:T(8,128)(2,1)S(1)} all-gather(bf16[24,1792]{1,0:T(8,128)(2,1)S(1)} %slice.24), channel_id=1, replica_groups=mesh['section'=32,'z'=12,'yl'=2] {'z'}, dimensions={0}, use_global_device_ids=true | all-gather | bytes 1118208 | tf_op jit(solution)/shard_map/all_gather | solution.py:175
  170.0 4.8 %collective-permute-start.4 = (bf16[288,1792]{1,0:T(8,128)(2,1)S(1)}, bf16[288,1792]{1,0:T(8,128)(2,1)S(1)}, u32[]{:S(2)}, u32[]{:S(2)}) collective-permute-start(bf16[288,1792]{1,0:T(8,128)(2,1)S(1)} %all_gather.6), channel_id=1, source_target_pairs={{0,1},{1,0},{2,3},{3,2},{4,5},{5,4},{6,7},{7,6},{8,9},{9,8},{10,11... | collective-permute-start | bytes 3096584 | tf_op jit(solution)/shard_map/ppermute | solution.py:176
  174.9 26.6 %all_gather.7 = bf16[288,1536]{1,0:T(8,128)(2,1)S(1)} all-gather(bf16[24,1536]{1,0:T(8,128)(2,1)S(1)} %pad_maximum_fusion.1), channel_id=1, replica_groups=mesh['section'=32,'z'=12,'yl'=2] {'z'}, dimensions={0}, use_global_device_ids=true | all-gather | bytes 958464 | tf_op jit(solution)/shard_map/all_gather | solution.py:178
  201.6 0.1 broadcast_select_fusion.1
  201.7 0.4 pad_maximum_fusion
  202.1 1.8 slice_bitcast_fusion
  203.9 1.1 copy.14
  (16 shorter events, 0.3 us)
Async XLA Ops:
  8.8 16.0 %copy-start = (bf16[288,2560]{1,0:T(8,128)(2,1)S(1)}, bf16[288,2560]{1,0:T(8,128)(2,1)}, u32[]{:S(2)}) copy-start(bf16[288,2560]{1,0:T(8,128)(2,1)} %get-tuple-element.15) | copy-start | bytes 4423684
  8.8 20.1 %copy-start.1 = (s32[1,1,18]{2,1,0:T(1,128)S(1)}, s32[1,1,18]{2,1,0:T(1,128)}, u32[]{:S(2)}) copy-start(s32[1,1,18]{2,1,0:T(1,128)} %param.14) | copy-start | bytes 220
  8.8 82.9 %all-to-all-start = ((bf16[24,8,5120]{2,1,0:T(8,128)(2,1)}), bf16[24,8,5120]{2,1,0:T(8,128)(2,1)S(1)}, u32[]{:S(2)}, u32[]{:S(2)}) async-start(bf16[24,8,5120]{2,1,0:T(8,128)(2,1)} %get-tuple-element.17), calls=%async_computation | async-start | bytes 3932160 | tf_op jit(solution)/shard_map/all_to_all | solution.py:159
  24.8 51.0 %collective-permute-start.1 = (bf16[288,2560]{1,0:T(8,128)(2,1)S(1)}, bf16[288,2560]{1,0:T(8,128)(2,1)S(1)}, u32[]{:S(2)}, u32[]{:S(2)}) collective-permute-start(bf16[288,2560]{1,0:T(8,128)(2,1)S(1)} %copy-done), channel_id=1, source_target_pairs={{0,1},{1,0},{2,3},{3,2},{4,5},{5,4},{6,7},{7,6},{8,9},{9,8},{10,11... | collective-permute-start | bytes 4423688 | tf_op jit(solution)/shard_map/ppermute | solution.py:160
  29.0 46.8 %collective-permute-start = (s32[19]{0:T(128)S(1)}, s32[19]{0:T(128)S(1)}, u32[]{:S(2)}, u32[]{:S(2)}) collective-permute-start(s32[19]{0:T(128)S(1)} %pad_add_fusion), channel_id=1, source_target_pairs={{0,24},{24,48},{48,72},{72,96},{96,120},{120,144},{144,168},{168,1... | collective-permute-start | bytes 236 | tf_op jit(solution)/shard_map/ppermute | solution.py:161
  94.5 49.0 %collective-permute-start.2 = (bf16[18,8,5120]{2,1,0:T(8,128)(2,1)S(1)}, bf16[18,8,5120]{2,1,0:T(8,128)(2,1)S(1)}, u32[]{:S(2)}, u32[]{:S(2)}) collective-permute-start(bf16[18,8,5120]{2,1,0:T(8,128)(2,1)S(1)} %compact.1), channel_id=1, source_target_pairs={{24,0},{48,24},{72,48},{96,72},{120,96},{144,120},{168,144},{192,1... | collective-permute-start | bytes 4423688 | tf_op jit(solution)/shard_map/ppermute | solution.py:164
  133.5 7.5 %collective-permute-start.5 = (bf16[11,4096]{1,0:T(8,128)(2,1)S(1)}, bf16[11,4096]{1,0:T(8,128)(2,1)S(1)}, u32[]{:S(2)}, u32[]{:S(2)}) collective-permute-start(bf16[11,4096]{1,0:T(8,128)(2,1)S(1)} %slice.30), channel_id=1, source_target_pairs={{0,2},{2,4},{4,6},{6,8},{8,10},{10,12},{12,14},{14,16},{16,18},{18... | collective-permute-start | bytes 270344
  141.6 33.3 %collective-permute-start.3 = (bf16[24,768]{1,0:T(8,128)(2,1)S(1)}, bf16[24,768]{1,0:T(8,128)(2,1)S(1)}, u32[]{:S(2)}, u32[]{:S(2)}) collective-permute-start(bf16[24,768]{1,0:T(8,128)(2,1)S(1)} %slice.25), channel_id=1, source_target_pairs={{0,1},{1,0},{2,3},{3,2},{4,5},{5,4},{6,7},{7,6},{8,9},{9,8},{10,11... | collective-permute-start | bytes 110600 | tf_op jit(solution)/shard_map/ppermute | solution.py:170
  170.0 31.6 %collective-permute-start.4 = (bf16[288,1792]{1,0:T(8,128)(2,1)S(1)}, bf16[288,1792]{1,0:T(8,128)(2,1)S(1)}, u32[]{:S(2)}, u32[]{:S(2)}) collective-permute-start(bf16[288,1792]{1,0:T(8,128)(2,1)S(1)} %all_gather.6), channel_id=1, source_target_pairs={{0,1},{1,0},{2,3},{3,2},{4,5},{5,4},{6,7},{7,6},{8,9},{9,8},{10,11... | collective-permute-start | bytes 3096584 | tf_op jit(solution)/shard_map/ppermute | solution.py:176

commit v4 on v3

--- a/solution.py
+++ b/solution.py
@@ -23,10 +23,10 @@
     return [slice(c, c + step) for c in range(0, width, step)]
 
 
-def _local(
-    y_ref, recv_ref, live_ref, gain, stash_hbm, back_in_hbm, down_hbm, up_hbm,
-    out_hbm, give_hbm, keep_hbm,
-    stash, back_in, down, up, mask, normed, out, give, keep, sems,
+def _cotangents(
+    recv_ref, live_ref, gain, stash_hbm, back_in_hbm, down_hbm, up_hbm,
+    out_hbm, normed_hbm, back_pre, activation,
+    stash, back_in, down, up, mask, normed, out, sems,
 ):
     f32, bf16 = jnp.float32, jnp.bfloat16
     pairs = ((stash_hbm, stash), (down_hbm, down), (back_in_hbm, back_in), (up_hbm, up))
@@ -53,47 +53,47 @@
         normed[:, cols] = n
         preact += lax.dot_general(n, down[:, cols], LAST, preferred_element_type=f32)
         back_act += lax.dot_general(back_in[:, cols], up[:, cols], LAST, preferred_element_type=f32)
+    stores = [pltpu.make_async_copy(normed, normed_hbm, sems.at[4])]
+    stores[0].start()
     sigmoid = 1.0 / (1.0 + jnp.exp(-preact))
-    act = (preact * sigmoid).astype(bf16)
+    activation[...] = (preact * sigmoid).astype(bf16)
     pre = (back_act * live * (sigmoid * (1.0 + preact * (1.0 - sigmoid)))).astype(bf16)
+    back_pre[...] = pre
     shared = jnp.sum(pre.astype(f32) * preact, axis=1, keepdims=True) * (inverse * (1.0 / D))
     alive = live > 0.5
-    for cols in _chunks(D, CHUNK):
-        back_norm = jnp.dot(pre, down[:, cols], preferred_element_type=f32) * gain[:, cols]
-        unit = stash[:, cols].astype(f32) * inverse
-        grad = back_in[:, cols].astype(f32) + inverse * back_norm - unit * shared
-        grad = jnp.where(alive, grad, 0.0)
-        for slot in range(SLOTS):
-            out[recv_ref[slot], :, cols] = grad[MB * slot : MB * (slot + 1), :].astype(bf16)
-    stores = [pltpu.make_async_copy(out, out_hbm, sems.at[4])]
-    stores[0].start()
-    y = y_ref[0]
-    for place, target, half in ((give, give_hbm, 1 - y), (keep, keep_hbm, y)):
-        for cols in _chunks(HALF, CHUNK):
-            here = pl.ds(pl.multiple_of(half * HALF + cols.start, 128), CHUNK)
-            place[:RANK, cols] = lax.dot_general(
-                pre, normed[:, here], FIRST, preferred_element_type=f32
-            ).astype(bf16)
-            place[RANK:, cols] = lax.dot_general(
-                act, back_in[:, here], FIRST, preferred_element_type=f32
-            ).astype(bf16)
-        stores.append(pltpu.make_async_copy(place, target, sems.at[4 + len(stores)]))
+    for half in range(2):
+        for part in _chunks(HALF, CHUNK):
+            cols = slice(half * HALF + part.start, half * HALF + part.stop)
+            back_norm = jnp.dot(pre, down[:, cols], preferred_element_type=f32) * gain[:, cols]
+            unit = stash[:, cols].astype(f32) * inverse
+            grad = back_in[:, cols].astype(f32) + inverse * back_norm - unit * shared
+            grad = jnp.where(alive, grad, 0.0)
+            for slot in range(SLOTS):
+                out[recv_ref[slot], :, cols] = grad[MB * slot : MB * (slot + 1), :].astype(bf16)
+        here = pl.ds(half * HALF, HALF)
+        stores.append(
+            pltpu.make_async_copy(out.at[:, :, here], out_hbm.at[:, :, here], sems.at[5 + half])
+        )
         stores[-1].start()
     for store in stores:
         store.wait()
 
 
-def local(y, recv, live, gain, stash, back_in, down, up):
+def cotangents(recv, live, gain, stash, back_in, down, up):
     smem = pl.BlockSpec(memory_space=pltpu.SMEM)
     vmem = pl.BlockSpec(memory_space=pltpu.VMEM)
     hbm = pl.BlockSpec(memory_space=pl.ANY)
     bf16 = jnp.bfloat16
-    outs = ((PEERS, MB, D), (2 * RANK, HALF), (2 * RANK, HALF))
     return pl.pallas_call(
-        _local,
-        out_shape=tuple(jax.ShapeDtypeStruct(shape, bf16) for shape in outs),
-        in_specs=[smem, smem, smem, vmem] + [hbm] * 4,
-        out_specs=[hbm] * 3,
+        _cotangents,
+        out_shape=(
+            jax.ShapeDtypeStruct((PEERS, MB, D), bf16),
+            jax.ShapeDtypeStruct((ROWS, D), bf16),
+            jax.ShapeDtypeStruct((ROWS, RANK), bf16),
+            jax.ShapeDtypeStruct((ROWS, RANK), bf16),
+        ),
+        in_specs=[smem, smem, vmem] + [hbm] * 4,
+        out_specs=[hbm, hbm, vmem, vmem],
         scratch_shapes=[
             pltpu.VMEM((ROWS, D), bf16),
             pltpu.VMEM((ROWS, D), bf16),
@@ -101,15 +101,48 @@
             pltpu.VMEM((RANK, D), bf16),
             pltpu.VMEM((ROWS, 128), jnp.float32),
             pltpu.VMEM((ROWS, D), bf16),
-        ]
-        + [pltpu.VMEM(shape, bf16) for shape in outs]
-        + [pltpu.SemaphoreType.DMA((7,))],
+            pltpu.VMEM((PEERS, MB, D), bf16),
+            pltpu.SemaphoreType.DMA((7,)),
+        ],
         compiler_params=pltpu.CompilerParams(vmem_limit_bytes=VMEM_LIMIT),
         cost_estimate=pl.CostEstimate(
-            flops=10 * ROWS * RANK * D, bytes_accessed=16 * ROWS * D, transcendentals=ROWS * RANK
-        ),
-        name="local",
-    )(y, recv, live, gain, stash, back_in, down, up)
+            flops=6 * ROWS * RANK * D, bytes_accessed=14 * ROWS * D, transcendentals=ROWS * RANK
+        ),
+        name="cotangents",
+    )(recv, live, gain, stash, back_in, down, up)
+
+
+def _gradients(y_ref, normed, back_in, back_pre, activation, give, keep):
+    f32, bf16 = jnp.float32, jnp.bfloat16
+    pre, act = back_pre[...], activation[...]
+    y = y_ref[0]
+    for out, half in ((give, 1 - y), (keep, y)):
+        for cols in _chunks(HALF, CHUNK):
+            here = pl.ds(pl.multiple_of(half * HALF + cols.start, 128), CHUNK)
+            out[:RANK, cols] = lax.dot_general(
+                pre, normed[:, here], FIRST, preferred_element_type=f32
+            ).astype(bf16)
+            out[RANK:, cols] = lax.dot_general(
+                act, back_in[:, here], FIRST, preferred_element_type=f32
+            ).astype(bf16)
+
+
+def gradients(y, normed, back_in, back_pre, activation):
+    vmem = pl.BlockSpec(memory_space=pltpu.VMEM)
+    return pl.pallas_call(
+        _gradients,
+        out_shape=(
+            jax.ShapeDtypeStruct((2 * RANK, HALF), jnp.bfloat16),
+            jax.ShapeDtypeStruct((2 * RANK, HALF), jnp.bfloat16),
+        ),
+        in_specs=[pl.BlockSpec(memory_space=pltpu.SMEM)] + [vmem] * 4,
+        out_specs=[vmem] * 2,
+        compiler_params=pltpu.CompilerParams(vmem_limit_bytes=VMEM_LIMIT),
+        cost_estimate=pl.CostEstimate(
+            flops=4 * ROWS * RANK * D, bytes_accessed=8 * ROWS * D, transcendentals=0
+        ),
+        name="gradients",
+    )(y, normed, back_in, back_pre, activation)
 
 
 def _compact(wiring, blocks, out, sems):
@@ -147,16 +180,18 @@
 def on_device(stash, back_in, down_proj, up_proj, gain, sent_to, sent_count, recv_from, back_live):
     f32, bf16 = jnp.float32, jnp.bfloat16
     y = lax.axis_index("yl")
+    side = y.astype(jnp.int32).reshape(1)
     swap = [(0, 1), (1, 0)]
     back = [((i + 1) % SECTIONS, i) for i in range(SECTIONS)]
     ahead = [(i, (i + 1) % SECTIONS) for i in range(SECTIONS)]
     stash = stash.reshape(ROWS, D)
     back_in = back_in.reshape(ROWS, D)
     live, recv = back_live[0, 0], recv_from[0, 0]
-    by_sender, give, keep = local(
-        y.astype(jnp.int32).reshape(1), recv, live, gain, stash, back_in, down_proj[0], up_proj[0]
+    by_sender, normed, back_pre, activation = cotangents(
+        recv, live, gain, stash, back_in, down_proj[0], up_proj[0]
     )
     exchanged = lax.all_to_all(by_sender, ("z", "yl"), split_axis=0, concat_axis=0, tiled=True)
+    give, keep = gradients(side, normed, back_in, back_pre, activation)
     got = lax.ppermute(give, "yl", swap)
     wiring = lax.ppermute(jnp.concatenate([sent_to[0, 0], sent_count[0]]), "section", ahead)
     keep, wiring = lax.optimization_barrier((keep, wiring))

time: 206 us -> 207 us (level)
  the two profiles are of different devices: /device:TPU:64 before, /device:TPU:32 now
where the time goes in v4:
time: 207 us; the launch traced here: 206 us
  blocking collectives  86.7 us (42%)
  waiting for transfers between devices  55.1 us (27%)
  starting transfers between devices  35.7 us (17%)
  Pallas kernels  13.9 us (7%)
  local copies, waits for them, and re-layouts  9.41 us (5%)
  other arithmetic  3.09 us (1%)
  between operations  2.13 us (1%)
    ppermute x1, waiting for transfers between devices, on_device(): lax.ppermute(jnp.concatenate([sent_to[0, 0], sent_count[0]]), 'section',...  47 us
    unnamed x1, blocking collectives  30.2 us
    all_gather x1, blocking collectives, on_device(): wide_mine = lax.all_gather(wide, 'z', axis=0, tiled=True)  28.8 us
    all_gather x1, blocking collectives, on_device(): narrow_all = lax.all_gather(narrow_both, 'z', axis=0, tiled=True)  27.7 us
    all_to_all x1, starting transfers between devices, on_device(): lax.all_to_all(by_sender, ('z', 'yl'), split_axis=0, concat_axis=0, tiled...  15.5 us
    all_to_all x1, waiting for transfers between devices, on_device(): lax.all_to_all(by_sender, ('z', 'yl'), split_axis=0, concat_axis=0, tiled...  8.08 us
    pallas_call x1, Pallas kernels, cotangents(): pl.pallas_call(_cotangents, out_shape=(jax.ShapeDtypeStruct((PEERS, MB, D...  7.4 us
    unnamed x1, starting transfers between devices  4.78 us
  transfers between devices with their start and end apart: 7, of which 2 were waited for; matrix products, arithmetic and copies ran while one was open for 19% of the time, Pallas kernels for 2%

profile of v4, /device:TPU:32, one launch (start us, length us, event | category | flops | bytes accessed | tf_op | source)
XLA Modules:
  0.0 206.0 jit_solution(7387500642386680085)
XLA Ops:
  0.6 7.4 %cotangents.1 = (bf16[24,8,5120]{2,1,0:T(8,128)(2,1)}, bf16[144,5120]{1,0:T(8,128)(2,1)}, bf16[144,144]{1,0:T(8,128)(2,1)}, bf16[144,144]{1,0:T(8,128)(2,1)}) custom-call(s32[18]{0:T(128)} %bitcast.24, s32[18]{0:T(128)} %bitcast.25, f32[1,5120]{1,0:T(1,128)} %gain.1, bf16[144,5120]{1,0:T(8,128)(2,1)} %bitcast.20, bf16[144,5120]{1,0:T(8,128)(2,1)} %bitcast.18, ...), custom_call_target="tpu_custom_call" | custom-call | flops 637009920 | bytes 10321920 | tf_op jit(solution)/shard_map/cotangents/pallas_call | solution.py:87
  8.0 15.5 %all-to-all-start = ((bf16[24,8,5120]{2,1,0:T(8,128)(2,1)}), bf16[24,8,5120]{2,1,0:T(8,128)(2,1)S(1)}, u32[]{:S(2)}, u32[]{:S(2)}) async-start(bf16[24,8,5120]{2,1,0:T(8,128)(2,1)} %get-tuple-element.23), calls=%async_computation | async-start | bytes 3932160 | tf_op jit(solution)/shard_map/all_to_all | solution.py:193
  23.6 4.0 %gradients.1 = (bf16[288,2560]{1,0:T(8,128)(2,1)}, bf16[288,2560]{1,0:T(8,128)(2,1)}) custom-call(s32[1]{0:T(128)} %bitcast.y_ref, bf16[144,5120]{1,0:T(8,128)(2,1)} %get-tuple-element.16.normed, bf16[144,5120]{1,0:T(8,128)(2,1)} %bitcast.19, bf16[144,144]{1,0:T(8,128)(2,1)} %get-tuple-element.17.back_pre, bf16[144,144]{1,0:T(8,128)(2,1)} %get-tuple-element.18.activation), custom_call_target="tpu_custom_call" | custom-call | flops 424673280 | bytes 5898240 | tf_op jit(solution)/shard_map/gradients/pallas_call | solution.py:132
  27.6 3.7 %collective-permute-start.1 = (bf16[288,2560]{1,0:T(8,128)(2,1)}, bf16[288,2560]{1,0:T(8,128)(2,1)S(1)}, u32[]{:S(2)}, u32[]{:S(2)}) collective-permute-start(bf16[288,2560]{1,0:T(8,128)(2,1)} %get-tuple-element.21), channel_id=1, source_target_pairs={{0,1},{1,0},{2,3},{3,2},{4,5},{5,4},{6,7},{7,6},{8,9},{9,8},{10,11... | collective-permute-start | bytes 4423688 | tf_op jit(solution)/shard_map/ppermute | solution.py:195
  32.0 1.9 collective-permute-start
  34.0 47.0 %collective-permute-done.wiring = s32[19]{0:T(128)S(1)} collective-permute-done((s32[19]{0:T(128)S(1)}, s32[19]{0:T(128)S(1)}, u32[]{:S(2)}, u32[]{:S(2)}) %collective-permute-start) | collective-permute-done | bytes 108 | tf_op jit(solution)/shard_map/ppermute | solution.py:196
  80.9 1.8 add_convert_fusion
  82.7 2.9 %reshape.27 = bf16[180,4096]{1,0:T(8,128)(2,1)} reshape(bf16[288,2560]{1,0:T(8,128)(2,1)S(1)} %add_convert_fusion) | data formatting | bytes 2949120 | tf_op jit(solution)/shard_map/reshape | solution.py:201
  85.6 8.1 %all-to-all-done.blocks = bf16[24,8,5120]{2,1,0:T(8,128)(2,1)S(1)} async-done(((bf16[24,8,5120]{2,1,0:T(8,128)(2,1)}), bf16[24,8,5120]{2,1,0:T(8,128)(2,1)S(1)}, u32[]{:S(2)}, u32[]{:S(2)}) %all-to-all-start) | async-done | bytes 1966112 | tf_op jit(solution)/shard_map/all_to_all | solution.py:193
  93.7 2.5 %compact.1 = bf16[18,8,5120]{2,1,0:T(8,128)(2,1)S(1)} custom-call(s32[19]{0:T(128)S(1)} %collective-permute-done.wiring, bf16[24,8,5120]{2,1,0:T(8,128)(2,1)S(1)} %all-to-all-done.blocks), custom_call_target="tpu_custom_call" | custom-call | bytes 3686400 | tf_op jit(solution)/shard_map/compact/pallas_call | solution.py:168
  96.2 4.3 %collective-permute-start.2 = (bf16[18,8,5120]{2,1,0:T(8,128)(2,1)S(1)}, bf16[18,8,5120]{2,1,0:T(8,128)(2,1)S(1)}, u32[]{:S(2)}, u32[]{:S(2)}) collective-permute-start(bf16[18,8,5120]{2,1,0:T(8,128)(2,1)S(1)} %compact.1), channel_id=1, source_target_pairs={{24,0},{48,24},{72,48},{96,72},{120,96},{144,120},{168,144},{192,1... | collective-permute-start | bytes 4423688 | tf_op jit(solution)/shard_map/ppermute | solution.py:199
  100.5 30.2 %fusion = bf16[16,4096]{1,0:T(8,128)(2,1)S(1)} fusion(bf16[180,4096]{1,0:T(8,128)(2,1)} %reshape.27), kind=kCustom, calls=%all-reduce-scatter | all-reduce-scatter fusion | flops 786433 | bytes 1609728
  130.7 4.8 %collective-permute-start.5 = (bf16[11,4096]{1,0:T(8,128)(2,1)S(1)}, bf16[11,4096]{1,0:T(8,128)(2,1)}, u32[]{:S(2)}, u32[]{:S(2)}) collective-permute-start(bf16[11,4096]{1,0:T(8,128)(2,1)S(1)} %slice.30), channel_id=1, source_target_pairs={{0,2},{2,4},{4,6},{6,8},{8,10},{10,12},{12,14},{14,16},{16,18},{18... | collective-permute-start | bytes 270344
  135.5 1.3 dynamic-slice.4
  137.4 1.2 concatenate.12
  138.7 0.7 multiply_convert_fusion
  139.4 1.1 reshape.28
  140.5 1.9 collective-permute-start.3
  142.4 28.8 %all_gather.6 = bf16[288,1792]{1,0:T(8,128)(2,1)S(1)} all-gather(bf16[24,1792]{1,0:T(8,128)(2,1)S(1)} %slice.24), channel_id=1, replica_groups=mesh['section'=32,'z'=12,'yl'=2] {'z'}, dimensions={0}, use_global_device_ids=true | all-gather | bytes 1118208 | tf_op jit(solution)/shard_map/all_gather | solution.py:210
  171.2 3.6 %collective-permute-start.4 = (bf16[288,1792]{1,0:T(8,128)(2,1)S(1)}, bf16[288,1792]{1,0:T(8,128)(2,1)S(1)}, u32[]{:S(2)}, u32[]{:S(2)}) collective-permute-start(bf16[288,1792]{1,0:T(8,128)(2,1)S(1)} %all_gather.6), channel_id=1, source_target_pairs={{0,1},{1,0},{2,3},{3,2},{4,5},{5,4},{6,7},{7,6},{8,9},{9,8},{10,11... | collective-permute-start | bytes 3096584 | tf_op jit(solution)/shard_map/ppermute | solution.py:211
  174.8 27.7 %all_gather.7 = bf16[288,1536]{1,0:T(8,128)(2,1)S(1)} all-gather(bf16[24,1536]{1,0:T(8,128)(2,1)S(1)} %pad_maximum_fusion.1), channel_id=1, replica_groups=mesh['section'=32,'z'=12,'yl'=2] {'z'}, dimensions={0}, use_global_device_ids=true | all-gather | bytes 958464 | tf_op jit(solution)/shard_map/all_gather | solution.py:213
  202.8 0.4 pad_maximum_fusion
  203.1 1.8 slice_bitcast_fusion
  204.9 1.1 copy.14
  (15 shorter events, 0.4 us)
Async XLA Ops:
  8.0 85.7 %all-to-all-start = ((bf16[24,8,5120]{2,1,0:T(8,128)(2,1)}), bf16[24,8,5120]{2,1,0:T(8,128)(2,1)S(1)}, u32[]{:S(2)}, u32[]{:S(2)}) async-start(bf16[24,8,5120]{2,1,0:T(8,128)(2,1)} %get-tuple-element.23), calls=%async_computation | async-start | bytes 3932160 | tf_op jit(solution)/shard_map/all_to_all | solution.py:193
  23.5 8.4 %copy-start = (s32[1,1,18]{2,1,0:T(1,128)S(1)}, s32[1,1,18]{2,1,0:T(1,128)}, u32[]{:S(2)}) copy-start(s32[1,1,18]{2,1,0:T(1,128)} %param.14) | copy-start | bytes 220
  27.6 53.4 %collective-permute-start.1 = (bf16[288,2560]{1,0:T(8,128)(2,1)}, bf16[288,2560]{1,0:T(8,128)(2,1)S(1)}, u32[]{:S(2)}, u32[]{:S(2)}) collective-permute-start(bf16[288,2560]{1,0:T(8,128)(2,1)} %get-tuple-element.21), channel_id=1, source_target_pairs={{0,1},{1,0},{2,3},{3,2},{4,5},{5,4},{6,7},{7,6},{8,9},{9,8},{10,11... | collective-permute-start | bytes 4423688 | tf_op jit(solution)/shard_map/ppermute | solution.py:195
  32.0 48.9 %collective-permute-start = (s32[19]{0:T(128)S(1)}, s32[19]{0:T(128)S(1)}, u32[]{:S(2)}, u32[]{:S(2)}) collective-permute-start(s32[19]{0:T(128)S(1)} %pad_add_fusion), channel_id=1, source_target_pairs={{0,24},{24,48},{48,72},{72,96},{96,120},{120,144},{144,168},{168,1... | collective-permute-start | bytes 236 | tf_op jit(solution)/shard_map/ppermute | solution.py:196
  96.2 46.2 %collective-permute-start.2 = (bf16[18,8,5120]{2,1,0:T(8,128)(2,1)S(1)}, bf16[18,8,5120]{2,1,0:T(8,128)(2,1)S(1)}, u32[]{:S(2)}, u32[]{:S(2)}) collective-permute-start(bf16[18,8,5120]{2,1,0:T(8,128)(2,1)S(1)} %compact.1), channel_id=1, source_target_pairs={{24,0},{48,24},{72,48},{96,72},{120,96},{144,120},{168,144},{192,1... | collective-permute-start | bytes 4423688 | tf_op jit(solution)/shard_map/ppermute | solution.py:199
  130.7 6.7 %collective-permute-start.5 = (bf16[11,4096]{1,0:T(8,128)(2,1)S(1)}, bf16[11,4096]{1,0:T(8,128)(2,1)}, u32[]{:S(2)}, u32[]{:S(2)}) collective-permute-start(bf16[11,4096]{1,0:T(8,128)(2,1)S(1)} %slice.30), channel_id=1, source_target_pairs={{0,2},{2,4},{4,6},{6,8},{8,10},{10,12},{12,14},{14,16},{16,18},{18... | collective-permute-start | bytes 270344
  140.5 34.4 %collective-permute-start.3 = (bf16[24,768]{1,0:T(8,128)(2,1)S(1)}, bf16[24,768]{1,0:T(8,128)(2,1)S(1)}, u32[]{:S(2)}, u32[]{:S(2)}) collective-permute-start(bf16[24,768]{1,0:T(8,128)(2,1)S(1)} %slice.25), channel_id=1, source_target_pairs={{0,1},{1,0},{2,3},{3,2},{4,5},{5,4},{6,7},{7,6},{8,9},{9,8},{10,11... | collective-permute-start | bytes 110600 | tf_op jit(solution)/shard_map/ppermute | solution.py:205
  171.2 31.4 %collective-permute-start.4 = (bf16[288,1792]{1,0:T(8,128)(2,1)S(1)}, bf16[288,1792]{1,0:T(8,128)(2,1)S(1)}, u32[]{:S(2)}, u32[]{:S(2)}) collective-permute-start(bf16[288,1792]{1,0:T(8,128)(2,1)S(1)} %all_gather.6), channel_id=1, source_target_pairs={{0,1},{1,0},{2,3},{3,2},{4,5},{5,4},{6,7},{7,6},{8,9},{9,8},{10,11... | collective-permute-start | bytes 3096584 | tf_op jit(solution)/shard_map/ppermute | solution.py:211
